TPU v7x, 32 devices: a whole 2x2x4 slice. The times are simulated.
32 devices in a mesh: group: 1, node: 8 (over z, core), dev: 4 (over y, x).
Axes of the slice: x: 2, y: 2, z: 4, core: 2. Of those that a mesh axis runs over, the one named last changes fastest.
Arguments:
- tokens: bfloat16 [4096, 2048], P(('group', 'node', 'dev')), may hold values from -6 to 6
- node_choice: int32 [4096, 4], P(('group', 'node', 'dev')), may hold values from 0 to 7, all different within a row; in each aligned block of 128 rows (0 to 127, 128 to 255, ...) at most 96 rows name the same one
- local_pick: int32 [4096, 4, 2], P(('group', 'node', 'dev')), may hold values from 0 to 3, all different within a row
- gate_scores: float32 [4096, 32], P(('group', 'node', 'dev')), may hold values from 0.1 to 2
- placement: int32 [32], replicated, may hold values from 0 to 31, as said below
- w_gate: bfloat16 [32, 2048, 768], P(('node', 'dev')), may hold values from -0.125 to 0.125
- w_up: bfloat16 [32, 2048, 768], P(('node', 'dev')), may hold values from -0.125 to 0.125
- w_down: bfloat16 [32, 768, 2048], P(('node', 'dev')), may hold values from -0.21875 to 0.21875
Outputs:
- mixed: bfloat16 [4096, 2048], P(('group', 'node', 'dev'))
Inputs may be any that keep to these rules, and one draw needn't show every extreme that they name: `placement`: the 4 experts g * 4 to g * 4 + 3 of group g sit on the 4 devices of one node, one expert a device; each device holds one expert. `node_choice`: each token names 4 different groups; among the tokens of one device no group is named by more than 96, a bound that some block reaches. `local_pick`: the 2 members taken in one group are different.
All inputs are finite; a program needn't handle non-finite values.
Results may differ from a plain program's by a relative error of at most 0.0085.
Values may be sent and summed in bfloat16 or wider, within the bound.
A program may use at most 128 MiB of HBM per device.

v0:
```python
import jax
import jax.numpy as jnp
from jax import lax
from jax.sharding import PartitionSpec as P


def expert_terms(slot_rows, slot_gates, gate_matrix, up_matrix, down_matrix):
    row_total = slot_rows.shape[0]
    width = slot_rows.shape[1]
    live_mask = slot_gates > 0
    live_int = live_mask.astype(jnp.int32)
    live_count = jnp.sum(live_int)
    live_before = jnp.cumsum(live_int) - live_int
    spare_before = jnp.arange(row_total, dtype=jnp.int32) - live_before
    position = jnp.where(live_mask, live_before, live_count + spare_before)
    block_rows = min(512, row_total)
    padded_rows = -(-row_total // block_rows) * block_rows
    packed = jnp.zeros((padded_rows, width), jnp.bfloat16).at[position].set(slot_rows)
    outputs = jnp.zeros((padded_rows, down_matrix.shape[1]), jnp.bfloat16)

    def one_block(block_index, outputs):
        first_row = block_index * block_rows
        row_block = lax.dynamic_slice_in_dim(packed, first_row, block_rows, 0)
        gate_part = jnp.dot(row_block, gate_matrix, preferred_element_type=jnp.float32)
        up_part = jnp.dot(row_block, up_matrix, preferred_element_type=jnp.float32)
        hidden = (jax.nn.silu(gate_part) * up_part).astype(jnp.bfloat16)
        result = jnp.dot(hidden, down_matrix, preferred_element_type=jnp.float32).astype(
            jnp.bfloat16
        )
        return lax.dynamic_update_slice_in_dim(outputs, result, first_row, 0)

    block_count = (live_count + block_rows - 1) // block_rows
    outputs = lax.fori_loop(0, block_count, one_block, outputs)
    restored = outputs[position]
    return (slot_gates.astype(jnp.float32)[:, None] * restored.astype(jnp.float32)).astype(
        jnp.bfloat16
    )


def arrival_ranks(targets, target_count):
    onehot = (targets[:, None] == jnp.arange(target_count, dtype=jnp.int32)).astype(jnp.int32)
    return jnp.sum(jnp.cumsum(onehot, axis=0) * onehot, axis=-1) - 1


def local(tokens, node_choice, local_pick, gate_scores, placement, w_gate, w_up, w_down):
    tok_count = tokens.shape[0]
    width = tokens.shape[1]
    groups_each = node_choice.shape[1]
    pair_each = local_pick.shape[2]
    node_count = lax.axis_size("node")
    dev_count = lax.axis_size("dev")
    expert_total = placement.shape[0]
    capacity = min(tok_count, max(2, 3 * tok_count * groups_each // (2 * node_count)))
    gate_matrix = w_gate[0]
    up_matrix = w_up[0]
    down_matrix = w_down[0]
    expert_ids = node_choice[:, :, None] * dev_count + local_pick
    matches = expert_ids[..., None] == jnp.arange(expert_total, dtype=jnp.int32)
    slot_ids = jnp.sum(jnp.where(matches, placement, 0), axis=-1)
    raw_scores = jnp.sum(jnp.where(matches, gate_scores[:, None, None, :], 0.0), axis=-1)
    gate_values = (raw_scores / jnp.sum(raw_scores, axis=(1, 2), keepdims=True)).astype(
        jnp.bfloat16
    )
    flat_slots = slot_ids.reshape(-1)
    slot_ranks = arrival_ranks(flat_slots, expert_total)
    target = flat_slots * capacity + slot_ranks
    pair_rows = jnp.broadcast_to(
        tokens[:, None, None, :], (tok_count, groups_each, pair_each, width)
    ).reshape(-1, width)
    send_rows = jnp.zeros((expert_total * capacity, width), jnp.bfloat16).at[target].set(pair_rows)
    send_gates = (
        jnp.zeros((expert_total * capacity,), jnp.bfloat16).at[target].set(gate_values.reshape(-1))
    )
    recv_rows, recv_gates = (
        lax.all_to_all(
            send_rows.reshape(expert_total, capacity, width),
            ("node", "dev"),
            split_axis=0,
            concat_axis=0,
            tiled=True,
        ),
        lax.all_to_all(
            send_gates.reshape(expert_total, capacity),
            ("node", "dev"),
            split_axis=0,
            concat_axis=0,
            tiled=True,
        ),
    )
    weighted = expert_terms(
        recv_rows.reshape(-1, width), recv_gates.reshape(-1), gate_matrix, up_matrix, down_matrix
    )
    returned = lax.all_to_all(
        weighted.reshape(expert_total, capacity, width),
        ("node", "dev"),
        split_axis=0,
        concat_axis=0,
        tiled=True,
    )
    pair_terms = returned.reshape(-1, width)[target].reshape(
        tok_count, groups_each, pair_each, width
    )
    node_part = jnp.sum(pair_terms.astype(jnp.float32), axis=2).astype(jnp.bfloat16)
    return jnp.sum(node_part.astype(jnp.float32), axis=1).astype(jnp.bfloat16)


def solution(mesh):
    return jax.shard_map(
        local,
        mesh=mesh,
        in_specs=(
            P(("group", "node", "dev"), None),
            P(("group", "node", "dev"), None),
            P(("group", "node", "dev"), None, None),
            P(("group", "node", "dev"), None),
            P(),
            P(("node", "dev"), None, None),
            P(("node", "dev"), None, None),
            P(("node", "dev"), None, None),
        ),
        out_specs=P(("group", "node", "dev"), None),
        check_vma=False,
    )
```

profile of v0, /device:TPU:0, one launch (start us, length us, event | category | flops | bytes accessed | tf_op | source)
XLA Modules:
  0.0 782.6 jit_solution(14919729706768426146)
XLA Ops:
  0.0 0.7 broadcast_multiply_fusion
  0.7 0.7 broadcast_add_fusion.3
  1.4 0.7 select_reduce_fusion.2
  2.1 0.2 copy.33
  2.3 0.2 eq.45
  2.6 0.2 eq.41
  2.8 0.8 select_reduce_fusion
  3.6 0.2 copy.38
  3.8 0.2 reshape.209
  4.0 9.0 %reduce-window.15 = s32[32,8,128]{2,1,0:T(8,128)S(1)} reduce-window(s32[32,8,128]{2,1,0:T(8,128)S(1)} %fusion.20, s32[]{:T(128)} %constant.47.clone.1), window={size=1x1x128 pad=0_0x0_0x127_0}, to_apply=%region_1.2 | reduce-window | flops 4161536 | bytes 262148 | tf_op jit(solution)/shard_map/reduce-window
  13.0 0.1 slice.21
  13.1 0.1 copy.35
  13.3 0.1 copy.36
  13.4 0.1 broadcast_add_fusion
  13.5 0.2 copy.32
  13.7 0.3 mul.49
  14.0 7.6 scatter_custom_fusion
  21.6 0.7 all_to_all.16
  22.3 7.5 all-to-all-start
  29.7 5.5 broadcast_in_dim.26
  35.3 7.2 reshape.217
  42.5 14.6 %scatter_custom_fusion.1 = bf16[3072,2048]{1,0:T(8,128)(2,1)} fusion(s32[1024]{0:T(1024)S(1)} %bitcast.48, bf16[1024,2048]{1,0:T(8,128)(2,1)} %reshape.217, bf16[]{:T(256)} %constant.45.clone.1), kind=kCustom, calls=%fused_computation.19 | custom fusion | bytes 12583424 | tf_op jit(solution)/shard_map/scatter | solution.py:70
  57.0 6.1 all-to-all-start.1
  63.1 0.7 fusion.21
  64.4 0.1 compare_reduce_fusion
  64.5 0.1 gt.18
  64.7 0.3 reduce-window.19
  65.0 0.1 slice.23
  65.1 0.1 slice_reduce_fusion
  65.2 0.1 broadcast_add_fusion.1
  65.3 0.7 compare_select_fusion
  66.0 281.4 %all-to-all-done.1 = bf16[32,96,2048]{2,1,0:T(8,128)(2,1)} async-done(((bf16[32,96,2048]{2,1,0:T(8,128)(2,1)}), bf16[32,96,2048]{2,1,0:T(8,128)(2,1)}, u32[]{:S(2)}, u32[]{:S(2)}) %all-to-all-start.1) | async-done | bytes 12582944 | tf_op jit(solution)/shard_map/all_to_all | solution.py:75
  347.4 25.7 %scatter_custom_fusion.2 = bf16[3072,2048]{1,0:T(8,128)(2,1)} fusion(s32[3072]{0:T(1024)S(1)} %bitcast.44, bf16[3072,2048]{1,0:T(8,128)(2,1)} %bitcast.8, bf16[]{:T(256)} %constant.45.clone.1), kind=kCustom, calls=%fused_computation.17 | custom fusion | bytes 12583424 | tf_op jit(solution)/shard_map/scatter | solution.py:18
  373.1 6.1 broadcast.127
  379.2 42.0 %while.10 = (s32[]{:T(128)}, bf16[3072,2048]{1,0:T(8,128)(2,1)}, s32[]{:T(128)}, bf16[3072,2048]{1,0:T(8,128)(2,1)}, bf16[2048,768]{1,0:T(8,128)(2,1)S(1)}, /*in...) while((s32[]{:T(128)}, bf16[3072,2048]{1,0:T(8,128)(2,1)}, ...), condition=%wide.region_13.14_spmd, body=%wide.region_12.13_spmd.sunk | while | flops 4835246080 | bytes 18875552 | solution.py:33
  379.6 4.7 fusion.41
  384.2 9.2 %fusion.42 = bf16[3072,2048]{1,0:T(8,128)(2,1)} fusion(bf16[3072,2048]{1,0:T(8,128)(2,1)} %get-tuple-element.118, s32[]{:T(128)S(6)} %select_n.64, bf16[768,2048]{1,0:T(8,128)(2,1)} %get-tuple-element.134, f32[512,768]{1,0:T(8,128)} %fusion.41, bf16[2048,768]{1,0:T(8,128)(2,1)} %get-tuple-element.133, bf16[3072,2048]{1,0:T(8,128)(2,1)} %get-tuple-element.131), kind=kOutput, calls=%fused_computation.6.clone.1 | convolution fusion | flops 3224633344 | bytes 12059648 | tf_op jit(solution)/shard_map/while/body/dot_general | solution.py:27
  393.4 4.6 fusion.41
  398.1 9.2 %fusion.42 = bf16[3072,2048]{1,0:T(8,128)(2,1)} fusion(bf16[3072,2048]{1,0:T(8,128)(2,1)} %get-tuple-element.118, s32[]{:T(128)S(6)} %select_n.64, bf16[768,2048]{1,0:T(8,128)(2,1)} %get-tuple-element.134, f32[512,768]{1,0:T(8,128)} %fusion.41, bf16[2048,768]{1,0:T(8,128)(2,1)} %get-tuple-element.133, bf16[3072,2048]{1,0:T(8,128)(2,1)} %get-tuple-element.131), kind=kOutput, calls=%fused_computation.6.clone.1 | convolution fusion | flops 3224633344 | bytes 12059648 | tf_op jit(solution)/shard_map/while/body/dot_general | solution.py:27
  407.3 4.6 fusion.41
  412.0 9.2 %fusion.42 = bf16[3072,2048]{1,0:T(8,128)(2,1)} fusion(bf16[3072,2048]{1,0:T(8,128)(2,1)} %get-tuple-element.118, s32[]{:T(128)S(6)} %select_n.64, bf16[768,2048]{1,0:T(8,128)(2,1)} %get-tuple-element.134, f32[512,768]{1,0:T(8,128)} %fusion.41, bf16[2048,768]{1,0:T(8,128)(2,1)} %get-tuple-element.133, bf16[3072,2048]{1,0:T(8,128)(2,1)} %get-tuple-element.131), kind=kOutput, calls=%fused_computation.6.clone.1 | convolution fusion | flops 3224633344 | bytes 12059648 | tf_op jit(solution)/shard_map/while/body/dot_general | solution.py:27
  421.2 30.0 %gather_fusion = bf16[3072,2048]{1,0:T(8,128)(2,1)} fusion(bf16[3072,2048]{1,0:T(8,128)(2,1)} %get-tuple-element.43, s32[3072]{0:T(1024)S(1)} %broadcast_clamp_fusion), kind=kCustom, calls=%fused_computation | custom fusion | bytes 25178112 | tf_op jit(solution)/shard_map/gather | solution.py:34
  451.2 11.2 %fusion.13 = bf16[32,96,2048]{2,1,0:T(8,128)(2,1)} fusion(bf16[32,96,2048]{2,1,0:T(8,128)(2,1)} %bitcast.40, f32[32,96]{1,0:T(8,128)S(1)} %bitcast.42), kind=kLoop, calls=%fused_computation.16 | loop fusion | flops 18874368 | bytes 25178112 | tf_op jit(solution)/shard_map/convert_element_type | solution.py:35
  462.4 3.9 all-to-all-start.2
  466.3 284.4 %all-to-all-done.2 = bf16[32,96,2048]{2,1,0:T(8,128)(2,1)} async-done(((bf16[32,96,2048]{2,1,0:T(8,128)(2,1)}), bf16[32,96,2048]{2,1,0:T(8,128)(2,1)}, u32[]{:S(2)}, u32[]{:S(2)}) %all-to-all-start.2) | async-done | bytes 12582944 | tf_op jit(solution)/shard_map/all_to_all | solution.py:93
  750.7 15.0 %gather_fusion.1 = bf16[1024,2048]{1,0:T(8,128)(2,1)} fusion(bf16[3072,2048]{1,0:T(8,128)(2,1)} %bitcast.13, s32[1024]{0:T(1024)S(1)} %broadcast_clamp_fusion.1), kind=kCustom, calls=%fused_computation.1 | custom fusion | bytes 8392704 | tf_op jit(solution)/shard_map/gather | solution.py:100
  765.7 7.6 reshape.185
  773.3 9.1 %reduce_sum.69 = bf16[128,2048]{1,0:T(8,128)(2,1)} reduce(bf16[128,4,2,2048]{3,2,1,0:T(2,128)(2,1)} %reshape.185, bf16[]{:T(256)} %constant.45.clone.1), dimensions={1,2}, to_apply=%region_14.15 | reduce | flops 1835008 | bytes 4718594 | tf_op jit(solution)/shard_map/reduce_sum | solution.py:104
  (16 shorter events, 0.3 us)
Async XLA Ops:
  22.3 34.8 %all-to-all-start = ((bf16[32,1,96]{2,1,0:T(2,128)(2,1)}), bf16[32,1,96]{2,1,0:T(2,128)(2,1)S(1)}, u32[]{:S(2)}, u32[]{:S(2)}) async-start(bf16[32,1,96]{2,1,0:T(2,128)(2,1)} %all_to_all.16), calls=%async_computation | async-start | bytes 32768 | tf_op jit(solution)/shard_map/all_to_all | solution.py:82
  57.0 290.3 %all-to-all-start.1 = ((bf16[32,96,2048]{2,1,0:T(8,128)(2,1)}), bf16[32,96,2048]{2,1,0:T(8,128)(2,1)}, u32[]{:S(2)}, u32[]{:S(2)}) async-start(bf16[32,96,2048]{2,1,0:T(8,128)(2,1)} %bitcast.39), calls=%async_computation.1 | async-start | bytes 25165824 | tf_op jit(solution)/shard_map/all_to_all | solution.py:75
  347.4 31.8 %copy-start = (bf16[1,2048,768]{2,1,0:T(8,128)(2,1)S(1)}, bf16[1,2048,768]{2,1,0:T(8,128)(2,1)}, u32[]{:S(2)}) copy-start(bf16[1,2048,768]{2,1,0:T(8,128)(2,1)} %param.15) | copy-start | bytes 9437188
  462.4 288.3 %all-to-all-start.2 = ((bf16[32,96,2048]{2,1,0:T(8,128)(2,1)}), bf16[32,96,2048]{2,1,0:T(8,128)(2,1)}, u32[]{:S(2)}, u32[]{:S(2)}) async-start(bf16[32,96,2048]{2,1,0:T(8,128)(2,1)} %fusion.13), calls=%async_computation.2 | async-start | bytes 25165824 | tf_op jit(solution)/shard_map/all_to_all | solution.py:93
where the time goes:
time: 791 us; the launch traced here: 783 us
  waiting for transfers between devices  566 us (72%)
  local copies, waits for them, and re-layouts  122 us (15%)
  matrix products  41.6 us (5%)
  other arithmetic  34.2 us (4%)
  starting transfers between devices  17.5 us (2%)
    all_to_all x1, waiting for transfers between devices, local(): lax.all_to_all(weighted.reshape(expert_total, capacity, width), ('node',...  284 us
    all_to_all x1, waiting for transfers between devices, local(): lax.all_to_all(send_rows.reshape(expert_total, capacity, width), ('node',...  281 us
    gather x1, local copies, waits for them, and re-layouts, expert_terms(): restored = outputs[position]  30 us
    dot_general x3, matrix products, one_block(): jnp.dot(hidden, down_matrix, preferred_element_type=jnp.float32)  27.7 us
    scatter x1, local copies, waits for them, and re-layouts, expert_terms(): jnp.zeros((padded_rows, width), jnp.bfloat16).at[position].set(slot_rows)  25.7 us
  transfers between devices with their start and end apart: 3, of which 2 were waited for; matrix products, arithmetic and copies ran while one was open for 4% of the time, Pallas kernels for 0%

commit v1 on v0

--- a/solution.py
+++ b/solution.py
@@ -1,7 +1,14 @@
+import functools
+
 import jax
 import jax.numpy as jnp
 from jax import lax
+from jax.experimental import pallas as pl
+from jax.experimental.pallas import tpu as pltpu
 from jax.sharding import PartitionSpec as P
+
+MESH = pl.DeviceIdType.MESH
+ROWS = 16
 
 
 def expert_terms(slot_rows, slot_gates, gate_matrix, up_matrix, down_matrix):
@@ -104,9 +111,391 @@
     return jnp.sum(node_part.astype(jnp.float32), axis=1).astype(jnp.bfloat16)
 
 
+def fused_kernel(layers, tok_ref, node_ref, pick_ref, score_ref, place_ref, wg_hbm, wu_hbm, wd_hbm,
+                 out_ref, held, spare, from_core, half_x, half_y, whole_x, whole_y, rise, fall,
+                 wg, wu, wd, hid, core_s, core_r, back_s, back_r, ax_s, ax_r, load_s):
+    tok, width = tok_ref.shape
+    half = tok // 2
+    n = lax.axis_index("node")
+    d = lax.axis_index("dev")
+    z, k = n // 2, n % 2
+    x, y = d % 2, d // 2
+    dx = y * 2 + (1 - x)
+    dy = (1 - y) * 2 + x
+    dd = (1 - y) * 2 + (1 - x)
+    mate = {"node": z * 2 + 1 - k, "dev": d}
+    to_x = {"node": n, "dev": dx}
+    to_y = {"node": n, "dev": dy}
+    up = {"node": n + 2, "dev": d}
+    down = {"node": n - 2, "dev": d}
+    has_up, has_down = z < layers - 1, z > 0
+    middle = ((z + 1) // 2) % 2
+
+    def near(j):
+        j = j + middle * (j // 2) * (5 - 2 * j)
+        return ((z // 2 + j // 2) % 2) * 2 + (z + j) % 2
+
+    loads = [
+        pltpu.make_async_copy(src.at[0], dst, load_s.at[i])
+        for i, (src, dst) in enumerate(((wg_hbm, wg), (wu_hbm, wu), (wd_hbm, wd)))
+    ]
+    for load in loads:
+        load.start()
+
+    experts = score_ref.shape[1]
+    lane = lax.broadcasted_iota(jnp.int32, (tok, experts), 1)
+    hit = jnp.zeros((tok, experts), jnp.float32)
+    groups, pair = node_ref.shape[1], pick_ref.shape[1] // node_ref.shape[1]
+    for g in range(groups):
+        for p in range(pair):
+            c = g * pair + p
+            expert = node_ref[:, g : g + 1] * 4 + pick_ref[:, c : c + 1]
+            hit = jnp.where(lane == expert, 1.0, hit)
+    raw = hit * score_ref[...]
+    gates = (raw / jnp.sum(raw, axis=1, keepdims=True)).astype(jnp.bfloat16)
+    mine = z * 4 + d
+    held[mine, 0, :, pl.ds(0, width)] = tok_ref[...]
+    held[mine, 0, :, pl.ds(width, 128)] = jnp.concatenate(
+        [gates, jnp.zeros((tok, 128 - experts), jnp.bfloat16)], axis=1
+    )
+
+    barrier = pltpu.get_barrier_semaphore()
+    for other in (mate, to_x, to_y):
+        pl.semaphore_signal(barrier, inc=1, device_id=other, device_id_type=MESH)
+
+    @pl.when(has_up)
+    def _():
+        pl.semaphore_signal(barrier, inc=1, device_id=up, device_id_type=MESH)
+
+    @pl.when(has_down)
+    def _():
+        pl.semaphore_signal(barrier, inc=1, device_id=down, device_id_type=MESH)
+
+    pl.semaphore_wait(barrier, 4 + middle)
+
+    def remote(src, dst, send, recv, to):
+        return pltpu.make_async_remote_copy(
+            src_ref=src, dst_ref=dst, send_sem=send, recv_sem=recv, device_id=to,
+            device_id_type=MESH,
+        )
+
+    def along(kind, zp, src, dst, to):
+        return remote(src, dst, ax_s.at[kind, zp], ax_r.at[kind, zp], to)
+
+    lo, hi = pl.ds(0, half), pl.ds(half, half)
+    cols = pl.ds(0, width)
+
+    def g_up(zp):
+        return along(0, zp, held.at[zp * 4 + d, 0], held.at[zp * 4 + d, 0], up)
+
+    def g_down(zp):
+        return along(1, zp, held.at[zp * 4 + d, 0], held.at[zp * 4 + d, 0], down)
+
+    def g_x(zp, dev):
+        return along(2, zp, held.at[zp * 4 + dev, 0], held.at[zp * 4 + dev, 0], to_x)
+
+    def g_y(zp, dev):
+        return along(3, zp, held.at[zp * 4 + dev, 0], held.at[zp * 4 + dev, 0], to_y)
+
+    def g_xh(zp, dev):
+        part = held.at[zp * 4 + dev, 0, hi]
+        return along(4, zp, part, part, to_x)
+
+    def g_yh(zp, dev):
+        part = held.at[zp * 4 + dev, 0, lo]
+        return along(5, zp, part, part, to_y)
+
+    def g_core(chip):
+        return remote(held.at[chip, 0], held.at[chip, 1], core_s.at[chip], core_r.at[chip], mate)
+
+    def b_core(chip):
+        return remote(spare.at[chip], from_core.at[chip], back_s.at[chip], back_r.at[chip], mate)
+
+    def b_xh(zp):
+        return along(6, zp, held.at[zp * 4 + dd, 1, lo, cols], half_x.at[zp], to_x)
+
+    def b_yh(zp):
+        return along(7, zp, held.at[zp * 4 + dd, 1, hi, cols], half_y.at[zp], to_y)
+
+    def b_x(zp):
+        return along(8, zp, held.at[zp * 4 + dx, 1, :, cols], whole_x.at[zp], to_x)
+
+    def b_y(zp):
+        return along(9, zp, held.at[zp * 4 + dy, 1, :, cols], whole_y.at[zp], to_y)
+
+    def b_up(zp):
+        return along(10, zp, held.at[zp * 4 + d, 1, :, cols], rise.at[zp], up)
+
+    def b_down(zp):
+        return along(11, zp, held.at[zp * 4 + d, 1, :, cols], fall.at[zp], down)
+
+    mask = (place_ref[...] == n * 4 + d).astype(jnp.float32)
+
+    def experts_of(chip):
+        def first(i, _):
+            at = pl.ds(pl.multiple_of(i * 256, 256), 256)
+            rows = held[chip, :, :, cols].reshape(2 * tok, width)
+            a = jnp.dot(rows, wg[:, at], preferred_element_type=jnp.float32)
+            b = jnp.dot(rows, wu[:, at], preferred_element_type=jnp.float32)
+            hid[:, at] = (a / (1.0 + jnp.exp(-a)) * b).astype(jnp.bfloat16)
+            return 0
+
+        lax.fori_loop(0, wg.shape[1] // 256, first, 0)
+        weights = held[chip, :, :, pl.ds(width, 128)].reshape(2 * tok, 128).astype(jnp.float32)
+        weight = jnp.sum(weights * mask, axis=1, keepdims=True)
+
+        def second(i, _):
+            at = pl.ds(pl.multiple_of(i * 256, 256), 256)
+            got = jnp.dot(hid[...], wd[:, at], preferred_element_type=jnp.float32)
+            term = (weight * got.astype(jnp.bfloat16).astype(jnp.float32)).astype(jnp.bfloat16)
+            held[chip, 1, :, at] = term[:tok]
+            spare[chip, :, at] = term[tok:]
+            return 0
+
+        lax.fori_loop(0, width // 256, second, 0)
+
+    def gather_step(t, _):
+        @pl.when(t < layers)
+        def _():
+            zp = near(t)
+
+            @pl.when(zp < z)
+            def _():
+                g_up(zp).wait_recv()
+
+            @pl.when(zp > z)
+            def _():
+                g_down(zp).wait_recv()
+
+            @pl.when(jnp.logical_and(zp <= z, has_up))
+            def _():
+                g_up(zp).start()
+
+            @pl.when(jnp.logical_and(zp >= z, has_down))
+            def _():
+                g_down(zp).start()
+
+            g_x(zp, d).start()
+            g_y(zp, d).start()
+            g_core(zp * 4 + d).start()
+
+        @pl.when(jnp.logical_and(t >= 1, t < layers + 1))
+        def _():
+            zp = near(t - 1)
+            g_x(zp, dx).wait_recv()
+            g_yh(zp, dx).start()
+            g_core(zp * 4 + dx).start()
+            g_y(zp, dy).wait_recv()
+            g_xh(zp, dy).start()
+            g_core(zp * 4 + dy).start()
+
+        @pl.when(t >= 2)
+        def _():
+            zp = near(t - 2)
+            g_xh(zp, dd).wait_recv()
+            g_yh(zp, dd).wait_recv()
+            g_core(zp * 4 + dd).start()
+
+        @pl.when(t == 0)
+        def _():
+            for load in loads:
+                load.wait()
+
+        def work(c, _):
+            j = t - (c + 1) // 2
+
+            @pl.when(jnp.logical_and(j >= 0, j < layers))
+            def _():
+                cx, cy = (x + c) % 2, (y + c // 2) % 2
+                chip = near(j) * 4 + cy * 2 + cx
+                g_core(chip).wait_recv()
+                experts_of(chip)
+                b_core(chip).start()
+
+            return 0
+
+        lax.fori_loop(0, 4, work, 0)
+        return 0
+
+    lax.fori_loop(0, layers + 2, gather_step, 0)
+
+    def total(chip, count, extra):
+        def rows(i, _):
+            at = pl.ds(pl.multiple_of(i * ROWS, ROWS), ROWS)
+            value = held[chip, 1, at, cols].astype(jnp.float32)
+            value = value + from_core[chip, at, :].astype(jnp.float32)
+            for ref, zp in extra:
+                value = value + ref[zp, at, :].astype(jnp.float32)
+            held[chip, 1, at, cols] = value.astype(jnp.bfloat16)
+            return 0
+
+        lax.fori_loop(0, count // ROWS, rows, 0)
+
+    def more(chip, first, count, ref, zp):
+        def rows(i, _):
+            at = pl.ds(pl.multiple_of(i * ROWS, ROWS), ROWS)
+            to = pl.ds(pl.multiple_of(first + i * ROWS, ROWS), ROWS)
+            value = held[chip, 1, to, cols].astype(jnp.float32) + ref[zp, at, :].astype(jnp.float32)
+            held[chip, 1, to, cols] = value.astype(jnp.bfloat16)
+            return 0
+
+        lax.fori_loop(0, count // ROWS, rows, 0)
+
+    def back_step(u, _):
+        @pl.when(u < layers)
+        def _():
+            zp = near(layers - 1 - u)
+            chip = zp * 4 + dd
+            b_core(chip).wait_recv()
+            total(chip, tok, ())
+            b_xh(zp).start()
+            b_yh(zp).start()
+
+        @pl.when(jnp.logical_and(u >= 1, u < layers + 1))
+        def _():
+            zp = near(layers - u)
+            b_core(zp * 4 + dx).wait_recv()
+            total(zp * 4 + dx, tok, ())
+            b_yh(zp).wait_recv()
+            more(zp * 4 + dx, half, half, half_y, zp)
+            b_x(zp).start()
+            b_core(zp * 4 + dy).wait_recv()
+            total(zp * 4 + dy, tok, ())
+            b_xh(zp).wait_recv()
+            more(zp * 4 + dy, 0, half, half_x, zp)
+            b_y(zp).start()
+
+        @pl.when(u >= 2)
+        def _():
+            zp = near(layers + 1 - u)
+            chip = zp * 4 + d
+            b_core(chip).wait_recv()
+            b_x(zp).wait_recv()
+            b_y(zp).wait_recv()
+            total(chip, tok, ((whole_x, zp), (whole_y, zp)))
+
+            @pl.when(jnp.logical_and(zp >= z, has_down))
+            def _():
+                b_up(zp).wait_recv()
+                more(chip, 0, tok, rise, zp)
+
+            @pl.when(jnp.logical_and(zp <= z, has_up))
+            def _():
+                b_down(zp).wait_recv()
+                more(chip, 0, tok, fall, zp)
+
+            @pl.when(zp > z)
+            def _():
+                b_up(zp).start()
+
+            @pl.when(zp < z)
+            def _():
+                b_down(zp).start()
+
+        return 0
+
+    lax.fori_loop(0, layers + 2, back_step, 0)
+    out_ref[...] = held[mine, 1, :, cols]
+
+    def drain(zp, _):
+        g_x(zp, d).wait_send()
+        g_y(zp, d).wait_send()
+        g_xh(zp, dy).wait_send()
+        g_yh(zp, dx).wait_send()
+        b_xh(zp).wait_send()
+        b_yh(zp).wait_send()
+        b_x(zp).wait_send()
+        b_y(zp).wait_send()
+
+        @pl.when(jnp.logical_and(zp <= z, has_up))
+        def _():
+            g_up(zp).wait_send()
+
+        @pl.when(jnp.logical_and(zp >= z, has_down))
+        def _():
+            g_down(zp).wait_send()
+
+        @pl.when(zp > z)
+        def _():
+            b_up(zp).wait_send()
+
+        @pl.when(zp < z)
+        def _():
+            b_down(zp).wait_send()
+
+        def chips(c, _):
+            g_core(zp * 4 + c).wait_send()
+            b_core(zp * 4 + c).wait_send()
+            return 0
+
+        lax.fori_loop(0, 4, chips, 0)
+        return 0
+
+    lax.fori_loop(0, layers, drain, 0)
+
+
+def fused(tokens, node_choice, local_pick, gate_scores, placement, w_gate, w_up, w_down):
+    tok, width = tokens.shape
+    hidden = w_gate.shape[2]
+    layers = lax.axis_size("node") // 2
+    chips = layers * 4
+    place = jnp.pad(placement, (0, 128 - placement.shape[0]), constant_values=-1)[None, :]
+    vmem = pl.BlockSpec(memory_space=pltpu.VMEM)
+    any_space = pl.BlockSpec(memory_space=pl.ANY)
+    bf16 = jnp.bfloat16
+    dma = pltpu.SemaphoreType.DMA
+    return pl.pallas_call(
+        functools.partial(fused_kernel, layers),
+        out_shape=jax.ShapeDtypeStruct((tok, width), bf16),
+        in_specs=[vmem] * 5 + [any_space] * 3,
+        out_specs=vmem,
+        scratch_shapes=[
+            pltpu.VMEM((chips, 2, tok, width + 128), bf16),
+            pltpu.VMEM((chips, tok, width), bf16),
+            pltpu.VMEM((chips, tok, width), bf16),
+            pltpu.VMEM((layers, tok // 2, width), bf16),
+            pltpu.VMEM((layers, tok // 2, width), bf16),
+            pltpu.VMEM((layers, tok, width), bf16),
+            pltpu.VMEM((layers, tok, width), bf16),
+            pltpu.VMEM((layers, tok, width), bf16),
+            pltpu.VMEM((layers, tok, width), bf16),
+            pltpu.VMEM((width, hidden), bf16),
+            pltpu.VMEM((width, hidden), bf16),
+            pltpu.VMEM((hidden, width), bf16),
+            pltpu.VMEM((2 * tok, hidden), bf16),
+            dma((chips,)),
+            dma((chips,)),
+            dma((chips,)),
+            dma((chips,)),
+            dma((12, layers)),
+            dma((12, layers)),
+            dma((3,)),
+        ],
+        compiler_params=pltpu.CompilerParams(
+            collective_id=0, has_side_effects=True, vmem_limit_bytes=61 * 2**20
+        ),
+        cost_estimate=pl.CostEstimate(
+            flops=6 * 2 * chips * tok * width * hidden,
+            bytes_accessed=6 * width * hidden,
+            transcendentals=2 * chips * tok * hidden,
+        ),
+        name="fused_experts",
+    )(
+        tokens,
+        node_choice,
+        local_pick.reshape(tok, -1),
+        gate_scores,
+        place,
+        w_gate,
+        w_up,
+        w_down,
+    )
+
+
 def solution(mesh):
+    small = mesh.shape["node"] == 8 and mesh.shape["dev"] == 4
     return jax.shard_map(
-        local,
+        fused if small else local,
         mesh=mesh,
         in_specs=(
             P(("group", "node", "dev"), None),

time: 791 us -> 194 us (0.25); the launches traced: 783 us -> 194 us
  waiting for transfers between devices: 566 us -> 0 us
  Pallas kernels: 0 us -> 187 us
  local copies, waits for them, and re-layouts: 122 us -> 7.31 us
  matrix products: 41.6 us -> 0 us
  other arithmetic: 34.2 us -> 0 us
  starting transfers between devices: 17.5 us -> 0 us
    all_to_all x3 -> x0, waiting for transfers between devices: 566 us -> none  [the longest x1 284 us: local(): lax.all_to_all(weighted.reshape(expert_total, capacity, width), ('node',...]
    pallas_call x0 -> x1, Pallas kernels: none -> 187 us  [fused(): pl.pallas_call(functools.partial(fused_kernel, layers), out_shape=jax.Sha...]
    scatter x3 -> x0, local copies, waits for them, and re-layouts: 47.9 us -> none  [the longest x1 25.7 us: expert_terms(): jnp.zeros((padded_rows, width), jnp.bfloat16).at[position].set(slot_rows)]
    gather x2 -> x0, local copies, waits for them, and re-layouts: 45 us -> none  [the longest x1 30 us: expert_terms(): restored = outputs[position]]
    dot_general x6 -> x0, matrix products: 41.6 us -> none  [the longest x3 27.7 us: one_block(): jnp.dot(hidden, down_matrix, preferred_element_type=jnp.float32)]
    all_to_all x3 -> x0, starting transfers between devices: 17.5 us -> none  [the longest x1 7.47 us: local(): lax.all_to_all(send_gates.reshape(expert_total, capacity), ('node', 'dev'...]
    reshape x2 -> x1, local copies, waits for them, and re-layouts: 14.8 us -> 1.41 us  [fused(): local_pick.reshape(tok, -1)]
    convert_element_type x5 -> x0, other arithmetic: 11.9 us -> none  [the longest x1 11.2 us: expert_terms(): (slot_gates.astype(jnp.float32)[:, None] * restored.astype(jnp.float32))....]
  transfers between devices with their start and end apart: 3 -> 0, of which waited for: 2 -> 0; matrix products, arithmetic and copies ran while one was open for 4% -> 0% of each run, Pallas kernels for 0% -> 0%
where the time goes in v1:
time: 194 us
  Pallas kernels  187 us (96%)
  local copies, waits for them, and re-layouts  7.31 us (4%)
    pallas_call x1, Pallas kernels, fused(): pl.pallas_call(functools.partial(fused_kernel, layers), out_shape=jax.Sha...  187 us
    unnamed x3, local copies, waits for them, and re-layouts  4.73 us

profile of v1, /device:TPU:0, one launch (start us, length us, event | category | flops | bytes accessed | tf_op | source)
XLA Modules:
  0.0 193.8 jit_solution(17545527241311949850)
XLA Ops:
  0.0 1.2 pad_bitcast_fusion.place_ref
  1.2 1.4 copy.12.node_ref
  2.6 1.4 copy.13.pick_ref
  4.0 1.4 copy.14.score_ref
  5.4 186.5 %fused_experts.1 = bf16[128,2048]{1,0:T(8,128)(2,1)} custom-call(bf16[128,2048]{1,0:T(8,128)(2,1)} %tok_ref.1, s32[128,4]{1,0:T(8,128)} %copy.12.node_ref, s32[128,8]{1,0:T(8,128)} %copy.13.pick_ref, f32[128,32]{1,0:T(8,128)} %copy.14.score_ref, s32[1,128]{1,0:T(1,128)} %pad_bitcast_fusion.place_ref, bf16[1,2048,768]{2,1,0:T(8,128)(2,1)} %wg_hbm.1, ...), custom_call_target="tpu_custom_call" | custom-call | flops 38654705664 | bytes 9437184 | tf_op jit(solution)/shard_map/fused_experts/pallas_call | solution.py:447
  191.9 1.9 copy.16

commit v2 on v1

--- a/solution.py
+++ b/solution.py
@@ -112,7 +112,7 @@
 
 
 def fused_kernel(layers, tok_ref, node_ref, pick_ref, score_ref, place_ref, wg_hbm, wu_hbm, wd_hbm,
-                 out_ref, held, spare, from_core, half_x, half_y, whole_x, whole_y, rise, fall,
+                 out_ref, held, spare, from_core, half_x, half_y, whole_x, whole_y, from_z, from_layer,
                  wg, wu, wd, hid, core_s, core_r, back_s, back_r, ax_s, ax_r, load_s):
     tok, width = tok_ref.shape
     half = tok // 2
@@ -128,6 +128,7 @@
     to_y = {"node": n, "dev": dy}
     up = {"node": n + 2, "dev": d}
     down = {"node": n - 2, "dev": d}
+    to_z = {"node": (z + 1 - 2 * (z % 2)) * 2 + k, "dev": d}
     has_up, has_down = z < layers - 1, z > 0
     middle = ((z + 1) // 2) % 2
 
@@ -142,36 +143,25 @@
     for load in loads:
         load.start()
 
-    experts = score_ref.shape[1]
-    lane = lax.broadcasted_iota(jnp.int32, (tok, experts), 1)
-    hit = jnp.zeros((tok, experts), jnp.float32)
-    groups, pair = node_ref.shape[1], pick_ref.shape[1] // node_ref.shape[1]
-    for g in range(groups):
-        for p in range(pair):
-            c = g * pair + p
-            expert = node_ref[:, g : g + 1] * 4 + pick_ref[:, c : c + 1]
-            hit = jnp.where(lane == expert, 1.0, hit)
+    experts = score_ref.shape[0]
+    row = lax.broadcasted_iota(jnp.int32, (experts, tok), 0)
+    hit = jnp.zeros((experts, tok), jnp.float32)
+    for g in range(pick_ref.shape[0]):
+        for p in range(pick_ref.shape[1]):
+            expert = node_ref[g : g + 1, :] * 4 + pick_ref[g, p : p + 1, :]
+            hit = jnp.where(row == expert, 1.0, hit)
     raw = hit * score_ref[...]
-    gates = (raw / jnp.sum(raw, axis=1, keepdims=True)).astype(jnp.bfloat16)
+    gates = raw / jnp.sum(raw, axis=0, keepdims=True)
+    gates = jnp.concatenate([gates, jnp.zeros((128 - experts, tok), jnp.float32)], axis=0)
     mine = z * 4 + d
     held[mine, 0, :, pl.ds(0, width)] = tok_ref[...]
-    held[mine, 0, :, pl.ds(width, 128)] = jnp.concatenate(
-        [gates, jnp.zeros((tok, 128 - experts), jnp.bfloat16)], axis=1
-    )
+    held[mine, 0, :, pl.ds(width, 128)] = gates.T.astype(jnp.bfloat16)
 
     barrier = pltpu.get_barrier_semaphore()
-    for other in (mate, to_x, to_y):
+    layer_of = [{"node": ((z + i) % layers) * 2 + k, "dev": d} for i in range(1, layers)]
+    for other in [mate, to_x, to_y] + layer_of:
         pl.semaphore_signal(barrier, inc=1, device_id=other, device_id_type=MESH)
-
-    @pl.when(has_up)
-    def _():
-        pl.semaphore_signal(barrier, inc=1, device_id=up, device_id_type=MESH)
-
-    @pl.when(has_down)
-    def _():
-        pl.semaphore_signal(barrier, inc=1, device_id=down, device_id_type=MESH)
-
-    pl.semaphore_wait(barrier, 4 + middle)
+    pl.semaphore_wait(barrier, layers + 2)
 
     def remote(src, dst, send, recv, to):
         return pltpu.make_async_remote_copy(
@@ -205,6 +195,9 @@
         part = held.at[zp * 4 + dev, 0, lo]
         return along(5, zp, part, part, to_y)
 
+    def g_z(zp):
+        return along(6, zp, held.at[zp * 4 + dd, 0], held.at[zp * 4 + dd, 0], to_z)
+
     def g_core(chip):
         return remote(held.at[chip, 0], held.at[chip, 1], core_s.at[chip], core_r.at[chip], mate)
 
@@ -212,24 +205,28 @@
         return remote(spare.at[chip], from_core.at[chip], back_s.at[chip], back_r.at[chip], mate)
 
     def b_xh(zp):
-        return along(6, zp, held.at[zp * 4 + dd, 1, lo, cols], half_x.at[zp], to_x)
+        return along(7, zp, held.at[zp * 4 + dd, 1, lo, cols], half_x.at[zp], to_x)
 
     def b_yh(zp):
-        return along(7, zp, held.at[zp * 4 + dd, 1, hi, cols], half_y.at[zp], to_y)
+        return along(8, zp, held.at[zp * 4 + dd, 1, hi, cols], half_y.at[zp], to_y)
 
     def b_x(zp):
-        return along(8, zp, held.at[zp * 4 + dx, 1, :, cols], whole_x.at[zp], to_x)
+        return along(9, zp, held.at[zp * 4 + dx, 1, :, cols], whole_x.at[zp], to_x)
 
     def b_y(zp):
-        return along(9, zp, held.at[zp * 4 + dy, 1, :, cols], whole_y.at[zp], to_y)
-
-    def b_up(zp):
-        return along(10, zp, held.at[zp * 4 + d, 1, :, cols], rise.at[zp], up)
-
-    def b_down(zp):
-        return along(11, zp, held.at[zp * 4 + d, 1, :, cols], fall.at[zp], down)
-
-    mask = (place_ref[...] == n * 4 + d).astype(jnp.float32)
+        return along(10, zp, held.at[zp * 4 + dy, 1, :, cols], whole_y.at[zp], to_y)
+
+    def b_z(zp):
+        return along(11, zp, held.at[zp * 4 + dd, 1, :, cols], from_z.at[zp], to_z)
+
+    def b_layer(zp, source):
+        return remote(
+            held.at[zp * 4 + d, 1, :, cols], from_layer.at[source], ax_s.at[12, zp],
+            ax_r.at[12, source], {"node": zp * 2 + k, "dev": d},
+        )
+
+    here = (place_ref[...] == n * 4 + d).astype(jnp.float32)
+    mask = jnp.concatenate([here, jnp.zeros((1, 128 - experts), jnp.float32)], axis=1)
 
     def experts_of(chip):
         def first(i, _):
@@ -240,7 +237,7 @@
             hid[:, at] = (a / (1.0 + jnp.exp(-a)) * b).astype(jnp.bfloat16)
             return 0
 
-        lax.fori_loop(0, wg.shape[1] // 256, first, 0)
+        lax.fori_loop(0, wg.shape[1] // 256, first, 0, unroll=True)
         weights = held[chip, :, :, pl.ds(width, 128)].reshape(2 * tok, 128).astype(jnp.float32)
         weight = jnp.sum(weights * mask, axis=1, keepdims=True)
 
@@ -252,13 +249,26 @@
             spare[chip, :, at] = term[tok:]
             return 0
 
-        lax.fori_loop(0, width // 256, second, 0)
-
-    def gather_step(t, _):
-        @pl.when(t < layers)
-        def _():
-            zp = near(t)
-
+        lax.fori_loop(0, width // 256, second, 0, unroll=True)
+
+    def listed(q, act):
+        t, c = q // 5, q % 5
+        j = t - (c + 1) // 2 - c // 4
+
+        @pl.when(jnp.logical_and(j >= 0, j < layers))
+        def _():
+            zp = near(j)
+            other = (zp + z) % 2
+
+            @pl.when(jnp.logical_or(c < 3, c == 3 + other))
+            def _():
+                cx = (x + c % 2 + c // 4) % 2
+                cy = (y + c // 2 - c // 4) % 2
+                act(c, zp, zp * 4 + cy * 2 + cx)
+
+    def arrive(c, zp, chip):
+        @pl.when(c == 0)
+        def _():
             @pl.when(zp < z)
             def _():
                 g_up(zp).wait_recv()
@@ -277,47 +287,55 @@
 
             g_x(zp, d).start()
             g_y(zp, d).start()
-            g_core(zp * 4 + d).start()
-
-        @pl.when(jnp.logical_and(t >= 1, t < layers + 1))
-        def _():
-            zp = near(t - 1)
+
+        @pl.when(c == 1)
+        def _():
             g_x(zp, dx).wait_recv()
-            g_yh(zp, dx).start()
-            g_core(zp * 4 + dx).start()
+
+            @pl.when((zp + z) % 2 == 0)
+            def _():
+                g_yh(zp, dx).start()
+
+        @pl.when(c == 2)
+        def _():
             g_y(zp, dy).wait_recv()
-            g_xh(zp, dy).start()
-            g_core(zp * 4 + dy).start()
-
-        @pl.when(t >= 2)
-        def _():
-            zp = near(t - 2)
+
+            @pl.when((zp + z) % 2 == 0)
+            def _():
+                g_xh(zp, dy).start()
+
+        @pl.when(c == 3)
+        def _():
             g_xh(zp, dd).wait_recv()
             g_yh(zp, dd).wait_recv()
-            g_core(zp * 4 + dd).start()
-
-        @pl.when(t == 0)
+            g_z(zp).start()
+
+        @pl.when(c == 4)
+        def _():
+            g_z(zp).wait_recv()
+
+        g_core(chip).start()
+
+    def work(c, zp, chip):
+        g_core(chip).wait_recv()
+        experts_of(chip)
+        b_core(chip).start()
+
+    def gather_step(q, _):
+        listed(q, arrive)
+
+        @pl.when(q == 0)
         def _():
             for load in loads:
                 load.wait()
 
-        def work(c, _):
-            j = t - (c + 1) // 2
-
-            @pl.when(jnp.logical_and(j >= 0, j < layers))
-            def _():
-                cx, cy = (x + c) % 2, (y + c // 2) % 2
-                chip = near(j) * 4 + cy * 2 + cx
-                g_core(chip).wait_recv()
-                experts_of(chip)
-                b_core(chip).start()
-
-            return 0
-
-        lax.fori_loop(0, 4, work, 0)
+        @pl.when(q >= 1)
+        def _():
+            listed(q - 1, work)
+
         return 0
 
-    lax.fori_loop(0, layers + 2, gather_step, 0)
+    lax.fori_loop(0, 5 * (layers + 3) + 1, gather_step, 0)
 
     def total(chip, count, extra):
         def rows(i, _):
@@ -346,67 +364,102 @@
         def _():
             zp = near(layers - 1 - u)
             chip = zp * 4 + dd
-            b_core(chip).wait_recv()
-            total(chip, tok, ())
-            b_xh(zp).start()
-            b_yh(zp).start()
+
+            @pl.when((zp + z) % 2 == 1)
+            def _():
+                b_core(chip).wait_recv()
+                total(chip, tok, ())
+                b_z(zp).start()
 
         @pl.when(jnp.logical_and(u >= 1, u < layers + 1))
         def _():
             zp = near(layers - u)
+            chip = zp * 4 + dd
+
+            @pl.when((zp + z) % 2 == 0)
+            def _():
+                b_core(chip).wait_recv()
+                b_z(zp).wait_recv()
+                total(chip, tok, ((from_z, zp),))
+                b_xh(zp).start()
+                b_yh(zp).start()
+
+        @pl.when(jnp.logical_and(u >= 2, u < layers + 2))
+        def _():
+            zp = near(layers + 1 - u)
             b_core(zp * 4 + dx).wait_recv()
             total(zp * 4 + dx, tok, ())
-            b_yh(zp).wait_recv()
-            more(zp * 4 + dx, half, half, half_y, zp)
+
+            @pl.when((zp + z) % 2 == 0)
+            def _():
+                b_yh(zp).wait_recv()
+                more(zp * 4 + dx, half, half, half_y, zp)
+
             b_x(zp).start()
             b_core(zp * 4 + dy).wait_recv()
             total(zp * 4 + dy, tok, ())
-            b_xh(zp).wait_recv()
-            more(zp * 4 + dy, 0, half, half_x, zp)
+
+            @pl.when((zp + z) % 2 == 0)
+            def _():
+                b_xh(zp).wait_recv()
+                more(zp * 4 + dy, 0, half, half_x, zp)
+
             b_y(zp).start()
 
-        @pl.when(u >= 2)
-        def _():
-            zp = near(layers + 1 - u)
+        @pl.when(u >= 3)
+        def _():
+            zp = near(layers + 2 - u)
             chip = zp * 4 + d
             b_core(chip).wait_recv()
             b_x(zp).wait_recv()
             b_y(zp).wait_recv()
-            total(chip, tok, ((whole_x, zp), (whole_y, zp)))
-
-            @pl.when(jnp.logical_and(zp >= z, has_down))
-            def _():
-                b_up(zp).wait_recv()
-                more(chip, 0, tok, rise, zp)
-
-            @pl.when(jnp.logical_and(zp <= z, has_up))
-            def _():
-                b_down(zp).wait_recv()
-                more(chip, 0, tok, fall, zp)
-
-            @pl.when(zp > z)
-            def _():
-                b_up(zp).start()
-
-            @pl.when(zp < z)
-            def _():
-                b_down(zp).start()
+
+            @pl.when(u < layers + 2)
+            def _():
+                total(chip, tok, ((whole_x, zp), (whole_y, zp)))
+                b_layer(zp, z).start()
+
+            @pl.when(u == layers + 2)
+            def _():
+                sources = [near(i) for i in range(1, layers)]
+                for source in sources:
+                    b_layer(source, source).wait_recv()
+                total(
+                    chip, tok,
+                    [(whole_x, zp), (whole_y, zp)] + [(from_layer, source) for source in sources],
+                )
 
         return 0
 
-    lax.fori_loop(0, layers + 2, back_step, 0)
+    lax.fori_loop(0, layers + 3, back_step, 0)
     out_ref[...] = held[mine, 1, :, cols]
 
     def drain(zp, _):
         g_x(zp, d).wait_send()
         g_y(zp, d).wait_send()
-        g_xh(zp, dy).wait_send()
-        g_yh(zp, dx).wait_send()
-        b_xh(zp).wait_send()
-        b_yh(zp).wait_send()
         b_x(zp).wait_send()
         b_y(zp).wait_send()
 
+        @pl.when((zp + z) % 2 == 0)
+        def _():
+            g_xh(zp, dy).wait_send()
+            g_yh(zp, dx).wait_send()
+            g_z(zp).wait_send()
+            b_xh(zp).wait_send()
+            b_yh(zp).wait_send()
+
+        @pl.when((zp + z) % 2 == 1)
+        def _():
+            b_z(zp).wait_send()
+
+        @pl.when(zp < z)
+        def _():
+            b_layer(zp, z).wait_send()
+
+        @pl.when(zp > z)
+        def _():
+            b_layer(zp, z).wait_send()
+
         @pl.when(jnp.logical_and(zp <= z, has_up))
         def _():
             g_up(zp).wait_send()
@@ -414,14 +467,6 @@
         @pl.when(jnp.logical_and(zp >= z, has_down))
         def _():
             g_down(zp).wait_send()
-
-        @pl.when(zp > z)
-        def _():
-            b_up(zp).wait_send()
-
-        @pl.when(zp < z)
-        def _():
-            b_down(zp).wait_send()
 
         def chips(c, _):
             g_core(zp * 4 + c).wait_send()
@@ -439,7 +484,6 @@
     hidden = w_gate.shape[2]
     layers = lax.axis_size("node") // 2
     chips = layers * 4
-    place = jnp.pad(placement, (0, 128 - placement.shape[0]), constant_values=-1)[None, :]
     vmem = pl.BlockSpec(memory_space=pltpu.VMEM)
     any_space = pl.BlockSpec(memory_space=pl.ANY)
     bf16 = jnp.bfloat16
@@ -467,8 +511,8 @@
             dma((chips,)),
             dma((chips,)),
             dma((chips,)),
-            dma((12, layers)),
-            dma((12, layers)),
+            dma((13, layers)),
+            dma((13, layers)),
             dma((3,)),
         ],
         compiler_params=pltpu.CompilerParams(
@@ -482,10 +526,10 @@
         name="fused_experts",
     )(
         tokens,
-        node_choice,
-        local_pick.reshape(tok, -1),
-        gate_scores,
-        place,
+        node_choice.T,
+        local_pick.transpose(1, 2, 0),
+        gate_scores.T,
+        placement[None, :],
         w_gate,
         w_up,
         w_down,

time: 194 us -> 186 us (0.959)
  local copies, waits for them, and re-layouts: 7.31 us -> 1.88 us
  Pallas kernels: 187 us -> 183 us
    pallas_call x1, Pallas kernels: 187 us -> 183 us  [fused(): pl.pallas_call(functools.partial(fused_kernel, layers), out_shape=jax.Sha...]
    unnamed x3 -> x1, local copies, waits for them, and re-layouts: 4.73 us -> 1.88 us
where the time goes in v2:
time: 186 us; the launch traced here: 185 us
  Pallas kernels  183 us (98%)
  local copies, waits for them, and re-layouts  1.88 us (1%)
    pallas_call x1, Pallas kernels, fused(): pl.pallas_call(functools.partial(fused_kernel, layers), out_shape=jax.Sha...  183 us

profile of v2, /device:TPU:0, one launch (start us, length us, event | category | flops | bytes accessed | tf_op | source)
XLA Modules:
  0.0 185.2 jit_solution(16906429319074558009)
XLA Ops:
  0.0 183.3 %fused_experts.1 = bf16[128,2048]{1,0:T(8,128)(2,1)} custom-call(bf16[128,2048]{1,0:T(8,128)(2,1)} %tok_ref.1, s32[4,128]{1,0:T(4,128)} %bitcast.6, s32[4,2,128]{2,1,0:T(2,128)} %bitcast.5, f32[32,128]{1,0:T(8,128)} %bitcast.4, s32[1,32]{1,0:T(1,128)} %bitcast.7, bf16[1,2048,768]{2,1,0:T(8,128)(2,1)} %wg_hbm.1, bf16[1,2048,768]{2,1,0:T(8,128)(2,1)} %wu_hbm.1, ...), custom_call_target="tpu_custom_call" | custom-call | flops 38654705664 | bytes 9437184 | tf_op jit(solution)/shard_map/fused_experts/pallas_call | solution.py:491
  183.3 1.9 %copy.10 = bf16[128,2048]{1,0:T(8,128)(2,1)} copy(bf16[128,2048]{1,0:T(8,128)(2,1)} %fused_experts.1) | data formatting | bytes 1048576

commit v3 on v2

--- a/solution.py
+++ b/solution.py
@@ -112,7 +112,7 @@
 
 
 def fused_kernel(layers, tok_ref, node_ref, pick_ref, score_ref, place_ref, wg_hbm, wu_hbm, wd_hbm,
-                 out_ref, held, spare, from_core, half_x, half_y, whole_x, whole_y, from_z, from_layer,
+                 out_ref, held, spare, from_core, half_x, half_y, whole_x, whole_y, from_layer,
                  wg, wu, wd, hid, core_s, core_r, back_s, back_r, ax_s, ax_r, load_s):
     tok, width = tok_ref.shape
     half = tok // 2
@@ -128,7 +128,6 @@
     to_y = {"node": n, "dev": dy}
     up = {"node": n + 2, "dev": d}
     down = {"node": n - 2, "dev": d}
-    to_z = {"node": (z + 1 - 2 * (z % 2)) * 2 + k, "dev": d}
     has_up, has_down = z < layers - 1, z > 0
     middle = ((z + 1) // 2) % 2
 
@@ -195,9 +194,6 @@
         part = held.at[zp * 4 + dev, 0, lo]
         return along(5, zp, part, part, to_y)
 
-    def g_z(zp):
-        return along(6, zp, held.at[zp * 4 + dd, 0], held.at[zp * 4 + dd, 0], to_z)
-
     def g_core(chip):
         return remote(held.at[chip, 0], held.at[chip, 1], core_s.at[chip], core_r.at[chip], mate)
 
@@ -215,9 +211,6 @@
 
     def b_y(zp):
         return along(10, zp, held.at[zp * 4 + dy, 1, :, cols], whole_y.at[zp], to_y)
-
-    def b_z(zp):
-        return along(11, zp, held.at[zp * 4 + dd, 1, :, cols], from_z.at[zp], to_z)
 
     def b_layer(zp, source):
         return remote(
@@ -252,19 +245,13 @@
         lax.fori_loop(0, width // 256, second, 0, unroll=True)
 
     def listed(q, act):
-        t, c = q // 5, q % 5
-        j = t - (c + 1) // 2 - c // 4
+        t, c = q // 4, q % 4
+        j = t - (c + 1) // 2
 
         @pl.when(jnp.logical_and(j >= 0, j < layers))
         def _():
             zp = near(j)
-            other = (zp + z) % 2
-
-            @pl.when(jnp.logical_or(c < 3, c == 3 + other))
-            def _():
-                cx = (x + c % 2 + c // 4) % 2
-                cy = (y + c // 2 - c // 4) % 2
-                act(c, zp, zp * 4 + cy * 2 + cx)
+            act(c, zp, zp * 4 + (y + c // 2) % 2 * 2 + (x + c) % 2)
 
     def arrive(c, zp, chip):
         @pl.when(c == 0)
@@ -292,27 +279,18 @@
         def _():
             g_x(zp, dx).wait_recv()
 
-            @pl.when((zp + z) % 2 == 0)
-            def _():
-                g_yh(zp, dx).start()
+            g_yh(zp, dx).start()
 
         @pl.when(c == 2)
         def _():
             g_y(zp, dy).wait_recv()
 
-            @pl.when((zp + z) % 2 == 0)
-            def _():
-                g_xh(zp, dy).start()
+            g_xh(zp, dy).start()
 
         @pl.when(c == 3)
         def _():
             g_xh(zp, dd).wait_recv()
             g_yh(zp, dd).wait_recv()
-            g_z(zp).start()
-
-        @pl.when(c == 4)
-        def _():
-            g_z(zp).wait_recv()
 
         g_core(chip).start()
 
@@ -335,7 +313,7 @@
 
         return 0
 
-    lax.fori_loop(0, 5 * (layers + 3) + 1, gather_step, 0)
+    lax.fori_loop(0, 4 * (layers + 2) + 1, gather_step, 0)
 
     def total(chip, count, extra):
         def rows(i, _):
@@ -360,29 +338,15 @@
         lax.fori_loop(0, count // ROWS, rows, 0)
 
     def back_step(u, _):
-        @pl.when(u < layers)
-        def _():
-            zp = near(layers - 1 - u)
-            chip = zp * 4 + dd
-
-            @pl.when((zp + z) % 2 == 1)
-            def _():
-                b_core(chip).wait_recv()
-                total(chip, tok, ())
-                b_z(zp).start()
-
         @pl.when(jnp.logical_and(u >= 1, u < layers + 1))
         def _():
             zp = near(layers - u)
             chip = zp * 4 + dd
 
-            @pl.when((zp + z) % 2 == 0)
-            def _():
-                b_core(chip).wait_recv()
-                b_z(zp).wait_recv()
-                total(chip, tok, ((from_z, zp),))
-                b_xh(zp).start()
-                b_yh(zp).start()
+            b_core(chip).wait_recv()
+            total(chip, tok, ())
+            b_xh(zp).start()
+            b_yh(zp).start()
 
         @pl.when(jnp.logical_and(u >= 2, u < layers + 2))
         def _():
@@ -390,19 +354,15 @@
             b_core(zp * 4 + dx).wait_recv()
             total(zp * 4 + dx, tok, ())
 
-            @pl.when((zp + z) % 2 == 0)
-            def _():
-                b_yh(zp).wait_recv()
-                more(zp * 4 + dx, half, half, half_y, zp)
+            b_yh(zp).wait_recv()
+            more(zp * 4 + dx, half, half, half_y, zp)
 
             b_x(zp).start()
             b_core(zp * 4 + dy).wait_recv()
             total(zp * 4 + dy, tok, ())
 
-            @pl.when((zp + z) % 2 == 0)
-            def _():
-                b_xh(zp).wait_recv()
-                more(zp * 4 + dy, 0, half, half_x, zp)
+            b_xh(zp).wait_recv()
+            more(zp * 4 + dy, 0, half, half_x, zp)
 
             b_y(zp).start()
 
@@ -431,7 +391,7 @@
 
         return 0
 
-    lax.fori_loop(0, layers + 3, back_step, 0)
+    lax.fori_loop(1, layers + 3, back_step, 0)
     out_ref[...] = held[mine, 1, :, cols]
 
     def drain(zp, _):
@@ -440,17 +400,10 @@
         b_x(zp).wait_send()
         b_y(zp).wait_send()
 
-        @pl.when((zp + z) % 2 == 0)
-        def _():
-            g_xh(zp, dy).wait_send()
-            g_yh(zp, dx).wait_send()
-            g_z(zp).wait_send()
-            b_xh(zp).wait_send()
-            b_yh(zp).wait_send()
-
-        @pl.when((zp + z) % 2 == 1)
-        def _():
-            b_z(zp).wait_send()
+        g_xh(zp, dy).wait_send()
+        g_yh(zp, dx).wait_send()
+        b_xh(zp).wait_send()
+        b_yh(zp).wait_send()
 
         @pl.when(zp < z)
         def _():
@@ -499,7 +452,6 @@
             pltpu.VMEM((chips, tok, width), bf16),
             pltpu.VMEM((layers, tok // 2, width), bf16),
             pltpu.VMEM((layers, tok // 2, width), bf16),
-            pltpu.VMEM((layers, tok, width), bf16),
             pltpu.VMEM((layers, tok, width), bf16),
             pltpu.VMEM((layers, tok, width), bf16),
             pltpu.VMEM((layers, tok, width), bf16),

time: 186 us -> 169 us (0.909)
  Pallas kernels: 183 us -> 167 us
    pallas_call x1, Pallas kernels: 183 us -> 167 us  [fused(): pl.pallas_call(functools.partial(fused_kernel, layers), out_shape=jax.Sha...]
where the time goes in v3:
time: 169 us
  Pallas kernels  167 us (99%)
  local copies, waits for them, and re-layouts  1.88 us (1%)
    pallas_call x1, Pallas kernels, fused(): pl.pallas_call(functools.partial(fused_kernel, layers), out_shape=jax.Sha...  167 us

profile of v3, /device:TPU:0, one launch (start us, length us, event | category | flops | bytes accessed | tf_op | source)
XLA Modules:
  0.0 168.5 jit_solution(17488262939316137795)
XLA Ops:
  0.0 166.6 %fused_experts.1 = bf16[128,2048]{1,0:T(8,128)(2,1)} custom-call(bf16[128,2048]{1,0:T(8,128)(2,1)} %tok_ref.1, s32[4,128]{1,0:T(4,128)} %bitcast.6, s32[4,2,128]{2,1,0:T(2,128)} %bitcast.5, f32[32,128]{1,0:T(8,128)} %bitcast.4, s32[1,32]{1,0:T(1,128)} %bitcast.7, bf16[1,2048,768]{2,1,0:T(8,128)(2,1)} %wg_hbm.1, bf16[1,2048,768]{2,1,0:T(8,128)(2,1)} %wu_hbm.1, ...), custom_call_target="tpu_custom_call" | custom-call | flops 38654705664 | bytes 9437184 | tf_op jit(solution)/shard_map/fused_experts/pallas_call | solution.py:444
  166.6 1.9 %copy.10 = bf16[128,2048]{1,0:T(8,128)(2,1)} copy(bf16[128,2048]{1,0:T(8,128)(2,1)} %fused_experts.1) | data formatting | bytes 1048576
